TPU v7x, 32 devices: a whole 2x2x4 slice. The times are simulated.
32 devices in a mesh: dp: 2 (over x), ctx: 4 (over y, core), tp: 4 (over z).
Axes of the slice: x: 2, y: 2, z: 4, core: 2. Of those that a mesh axis runs over, the one named last changes fastest.
Arguments:
- tokens: bfloat16 [8192, 768], P(('dp', 'ctx')), may hold values from -6 to 6
- w_query: bfloat16 [768, 768], P('dp', 'tp'), may hold values from -0.3125 to 0.3125
- w_key: bfloat16 [768, 768], P('dp', 'tp'), may hold values from -0.3125 to 0.3125
- w_value: bfloat16 [768, 768], P('dp', 'tp'), may hold values from -0.21875 to 0.21875
- w_out: bfloat16 [768, 768], P('tp', 'dp'), may hold values from -1.75 to 1.75
- w_act: bfloat16 [768, 1152], P('dp', 'tp'), may hold values from -0.21875 to 0.21875
- w_up: bfloat16 [768, 1152], P('dp', 'tp'), may hold values from -0.21875 to 0.21875
- w_down: bfloat16 [1152, 768], P('tp', 'dp'), may hold values from -0.1875 to 0.1875
- gain_one: bfloat16 [768], P('dp'), may hold values from 0.5 to 1.5
- gain_two: bfloat16 [768], P('dp'), may hold values from 0.5 to 1.5
- cotangent: bfloat16 [8192, 768], P(('dp', 'ctx')), may hold values from -6 to 6
Outputs:
- outputs: bfloat16 [8192, 768], P(('dp', 'ctx', 'tp'))
- input_grad: bfloat16 [8192, 768], P(('dp', 'ctx', 'tp'))
- grad_query: float32 [768, 768], P('dp', 'tp')
- grad_key: float32 [768, 768], P('dp', 'tp')
- grad_value: float32 [768, 768], P('dp', 'tp')
- grad_out: float32 [768, 768], P('tp', 'dp')
- grad_act: float32 [768, 1152], P('dp', 'tp')
- grad_up: float32 [768, 1152], P('dp', 'tp')
- grad_down: float32 [1152, 768], P('tp', 'dp')
- grad_gain_one: float32 [768], P('dp')
- grad_gain_two: float32 [768], P('dp')
All inputs are finite; a program needn't handle non-finite values.
Results may differ from a plain program's by a relative error of at most 0.024.
Values may be sent and summed in bfloat16 or wider, within the bound.
A program may use at most 128 MiB of HBM per device.

v0:
```python
import math
import jax
import jax.numpy as jnp
from jax import lax
from jax.sharding import PartitionSpec as P

HEAD = 64
EPSILON = 1e-05
ROPE_BASE = 160000.0


def standardize(values_in):
    mean_value = jnp.mean(values_in, axis=-1, keepdims=True)
    centred = values_in - mean_value
    inverse = lax.rsqrt(jnp.mean(centred * centred, axis=-1, keepdims=True) + EPSILON)
    return (centred * inverse, inverse)


def norm_back(grad_hat, hat_values, inverse):
    mean_grad = jnp.mean(grad_hat, axis=-1, keepdims=True)
    mean_cross = jnp.mean(grad_hat * hat_values, axis=-1, keepdims=True)
    return inverse * (grad_hat - mean_grad - hat_values * mean_cross)


def rotate(tensor):
    half_size = tensor.shape[-1] // 2
    return jnp.concatenate([-tensor[..., half_size:], tensor[..., :half_size]], axis=-1)


def unrotate(tensor):
    half_size = tensor.shape[-1] // 2
    return jnp.concatenate([tensor[..., half_size:], -tensor[..., :half_size]], axis=-1)


def rotary(tensor, cosine_table, sine_table):
    return tensor * cosine_table + rotate(tensor) * sine_table


def rotary_back(tensor, cosine_table, sine_table):
    return tensor * cosine_table + unrotate(tensor * sine_table)


def tables(offset, length, head_size):
    position = (offset + jnp.arange(length)).astype(jnp.float32)
    frequency = ROPE_BASE ** (-jnp.arange(0, head_size, 2).astype(jnp.float32) / head_size)
    angles = position[:, None] * frequency[None, :]
    angles = jnp.concatenate([angles, angles], axis=1)
    return (jnp.cos(angles)[:, None, :], jnp.sin(angles)[:, None, :])


def gelu_parts(values_in):
    normal_cdf = 0.5 * (1.0 + lax.erf(values_in * (1.0 / math.sqrt(2.0))))
    density = jnp.exp(-0.5 * values_in * values_in) * (1.0 / math.sqrt(2.0 * math.pi))
    return (values_in * normal_cdf, normal_cdf + values_in * density)


def block_scores(query_block, key_block, factor):
    return (
        jnp.einsum("qhd,khd->hqk", query_block, key_block, preferred_element_type=jnp.float32)
        * factor
    )


def attend(queries, key_data, value_data, head_count):
    query_rows = queries.shape[0]
    key_rows = key_data.shape[0]
    query_step = math.gcd(query_rows, 512)
    factor = HEAD ** (-0.5)
    query_blocks = queries.reshape(query_rows // query_step, query_step, head_count, HEAD)
    key_all = key_data.reshape(key_rows, head_count, HEAD)
    value_all = value_data.reshape(key_rows, head_count, HEAD)

    def per_query(query_block):
        scores = block_scores(query_block, key_all, factor)
        log_total = jax.nn.logsumexp(scores, axis=-1)
        weights = jnp.exp(scores - log_total[:, :, None]).astype(jnp.bfloat16)
        accumulated = jnp.einsum(
            "hqk,khd->qhd", weights, value_all, preferred_element_type=jnp.float32
        )
        return (accumulated.reshape(query_step, head_count * HEAD), log_total.T)

    mixed_blocks, log_blocks = lax.map(per_query, query_blocks)
    return (
        mixed_blocks.reshape(query_rows, head_count * HEAD),
        log_blocks.reshape(query_rows, head_count),
    )


def attend_back(queries, grad_mixed, log_totals, totals, key_data, value_data, head_count):
    query_rows = queries.shape[0]
    key_rows = key_data.shape[0]
    query_step = math.gcd(query_rows, 512)
    key_step = math.gcd(key_rows, 1024)
    factor = HEAD ** (-0.5)
    query_blocks = queries.reshape(query_rows // query_step, query_step, head_count, HEAD)
    grad_blocks = grad_mixed.reshape(query_rows // query_step, query_step, head_count, HEAD)
    log_blocks = log_totals.reshape(query_rows // query_step, query_step, head_count)
    total_blocks = totals.reshape(query_rows // query_step, query_step, head_count)
    key_blocks = key_data.reshape(key_rows // key_step, key_step, head_count, HEAD)
    value_blocks = value_data.reshape(key_rows // key_step, key_step, head_count, HEAD)

    def per_query(running, block_item):
        key_accum, value_accum = running
        query_block, grad_block, log_block, total_block = block_item

        def per_key(query_accum, key_item):
            key_block, value_block, key_sum, value_sum = key_item
            scores = block_scores(query_block, key_block, factor)
            weights_full = jnp.exp(scores - log_block.T[:, :, None])
            value_sum = value_sum + jnp.einsum(
                "hqk,qhd->khd",
                weights_full.astype(jnp.bfloat16),
                grad_block,
                preferred_element_type=jnp.float32,
            )
            grad_probs = jnp.einsum(
                "qhd,khd->hqk", grad_block, value_block, preferred_element_type=jnp.float32
            )
            grad_scores = (factor * weights_full * (grad_probs - total_block.T[:, :, None])).astype(
                jnp.bfloat16
            )
            query_accum = query_accum + jnp.einsum(
                "hqk,khd->qhd", grad_scores, key_block, preferred_element_type=jnp.float32
            )
            key_sum = key_sum + jnp.einsum(
                "hqk,qhd->khd", grad_scores, query_block, preferred_element_type=jnp.float32
            )
            return (query_accum, (key_sum, value_sum))

        initial = jnp.zeros((query_step, head_count, HEAD), jnp.float32)
        query_accum, (key_accum, value_accum) = lax.scan(
            per_key, initial, (key_blocks, value_blocks, key_accum, value_accum)
        )
        return ((key_accum, value_accum), query_accum)

    zero_blocks = jnp.zeros(key_blocks.shape, jnp.float32)
    (key_accum, value_accum), query_accum = lax.scan(
        per_query, (zero_blocks, zero_blocks), (query_blocks, grad_blocks, log_blocks, total_blocks)
    )
    feature_count = head_count * HEAD
    return (
        query_accum.reshape(query_rows, feature_count),
        key_accum.reshape(key_rows, feature_count),
        value_accum.reshape(key_rows, feature_count),
    )


def owner_shares(
    query_grad,
    key_grad,
    value_grad,
    act_grad,
    up_grad,
    gain_first_grad,
    gain_second_grad,
    out_grad,
    down_grad,
):
    row_parts = (
        lax.psum_scatter(
            query_grad.astype(jnp.bfloat16), "dp", scatter_dimension=0, tiled=True
        ).astype(jnp.float32),
        lax.psum_scatter(
            key_grad.astype(jnp.bfloat16), "dp", scatter_dimension=0, tiled=True
        ).astype(jnp.float32),
        lax.psum_scatter(
            value_grad.astype(jnp.bfloat16), "dp", scatter_dimension=0, tiled=True
        ).astype(jnp.float32),
        lax.psum_scatter(
            act_grad.astype(jnp.bfloat16), "dp", scatter_dimension=0, tiled=True
        ).astype(jnp.float32),
        lax.psum_scatter(
            up_grad.astype(jnp.bfloat16), "dp", scatter_dimension=0, tiled=True
        ).astype(jnp.float32),
        lax.psum_scatter(
            gain_first_grad.astype(jnp.bfloat16), "dp", scatter_dimension=0, tiled=True
        ).astype(jnp.float32),
        lax.psum_scatter(
            gain_second_grad.astype(jnp.bfloat16), "dp", scatter_dimension=0, tiled=True
        ).astype(jnp.float32),
    )
    col_parts = (
        lax.psum_scatter(
            out_grad.astype(jnp.bfloat16), "dp", scatter_dimension=1, tiled=True
        ).astype(jnp.float32),
        lax.psum_scatter(
            down_grad.astype(jnp.bfloat16), "dp", scatter_dimension=1, tiled=True
        ).astype(jnp.float32),
    )
    return tuple(row_parts) + tuple(col_parts)


def context_total(query_grad, key_grad, value_grad, act_grad, up_grad, out_grad, down_grad):
    return tuple(
        (
            lax.psum(query_grad.astype(jnp.bfloat16), "ctx").astype(jnp.float32),
            lax.psum(key_grad.astype(jnp.bfloat16), "ctx").astype(jnp.float32),
            lax.psum(value_grad.astype(jnp.bfloat16), "ctx").astype(jnp.float32),
            lax.psum(act_grad.astype(jnp.bfloat16), "ctx").astype(jnp.float32),
            lax.psum(up_grad.astype(jnp.bfloat16), "ctx").astype(jnp.float32),
            lax.psum(out_grad.astype(jnp.bfloat16), "ctx").astype(jnp.float32),
            lax.psum(down_grad.astype(jnp.bfloat16), "ctx").astype(jnp.float32),
        )
    )


def local(
    tokens, w_query, w_key, w_value, w_out, w_act, w_up, w_down, gain_one, gain_two, cotangent
):
    tok_rows = tokens.shape[0]
    query_w, key_w, value_w, act_w, up_w, gain_first, gain_second = (
        lax.all_gather(w_query, "dp", axis=0, tiled=True),
        lax.all_gather(w_key, "dp", axis=0, tiled=True),
        lax.all_gather(w_value, "dp", axis=0, tiled=True),
        lax.all_gather(w_act, "dp", axis=0, tiled=True),
        lax.all_gather(w_up, "dp", axis=0, tiled=True),
        lax.all_gather(gain_one, "dp", axis=0, tiled=True),
        lax.all_gather(gain_two, "dp", axis=0, tiled=True),
    )
    out_w, down_w = (
        lax.all_gather(w_out, "dp", axis=1, tiled=True),
        lax.all_gather(w_down, "dp", axis=1, tiled=True),
    )
    head_count = query_w.shape[1] // HEAD
    feature_count = head_count * HEAD
    share_rows = tok_rows // lax.axis_size("tp")
    share_start = lax.axis_index("tp") * share_rows

    def own_rows(array_in):
        return lax.dynamic_slice_in_dim(array_in, share_start, share_rows, 0)

    cosine_table, sine_table = tables(lax.axis_index("ctx") * tok_rows, tok_rows, HEAD)
    gain_first_f = gain_first.astype(jnp.float32)
    gain_second_f = gain_second.astype(jnp.float32)
    inputs = tokens.astype(jnp.float32)
    hat_one, inverse_one = standardize(inputs)
    normed = (hat_one * gain_first_f).astype(jnp.bfloat16)
    query_pre = jnp.dot(normed, query_w, preferred_element_type=jnp.float32).reshape(
        tok_rows, head_count, HEAD
    )
    key_pre = jnp.dot(normed, key_w, preferred_element_type=jnp.float32).reshape(
        tok_rows, head_count, HEAD
    )
    queries = (
        rotary(query_pre, cosine_table, sine_table)
        .astype(jnp.bfloat16)
        .reshape(tok_rows, feature_count)
    )
    key_data = (
        rotary(key_pre, cosine_table, sine_table)
        .astype(jnp.bfloat16)
        .reshape(tok_rows, feature_count)
    )
    value_data = jnp.dot(normed, value_w, preferred_element_type=jnp.float32).astype(jnp.bfloat16)
    keys_all, values_all = (
        lax.all_gather(key_data, "ctx", axis=0, tiled=True),
        lax.all_gather(value_data, "ctx", axis=0, tiled=True),
    )
    mixed_full, log_totals = attend(
        queries.reshape(tok_rows, head_count, HEAD), keys_all, values_all, head_count
    )
    mixed_low = mixed_full.astype(jnp.bfloat16)
    middle = inputs + lax.psum(
        jnp.dot(mixed_low, out_w, preferred_element_type=jnp.float32).astype(jnp.bfloat16), "tp"
    ).astype(jnp.float32)
    hat_two, inverse_two = standardize(middle)
    normed_two = (hat_two * gain_second_f).astype(jnp.bfloat16)
    gate_in = jnp.dot(normed_two, act_w, preferred_element_type=jnp.float32)
    up_in = jnp.dot(normed_two, up_w, preferred_element_type=jnp.float32)
    active_in, derivative_in = gelu_parts(gate_in)
    hidden = (active_in * up_in).astype(jnp.bfloat16)
    outputs = middle + lax.psum(
        jnp.dot(hidden, down_w, preferred_element_type=jnp.float32).astype(jnp.bfloat16), "tp"
    ).astype(jnp.float32)
    out_rows = own_rows(outputs)
    grad_hidden = jnp.dot(cotangent, down_w.T, preferred_element_type=jnp.float32)
    grad_gate = (grad_hidden * up_in * derivative_in).astype(jnp.bfloat16)
    grad_upin = (grad_hidden * active_in).astype(jnp.bfloat16)
    down_grad = jnp.dot(hidden.T, cotangent, preferred_element_type=jnp.float32)
    act_grad = jnp.dot(normed_two.T, grad_gate, preferred_element_type=jnp.float32)
    up_grad = jnp.dot(normed_two.T, grad_upin, preferred_element_type=jnp.float32)
    grad_normed_two = lax.psum(
        (
            jnp.dot(grad_gate, act_w.T, preferred_element_type=jnp.float32)
            + jnp.dot(grad_upin, up_w.T, preferred_element_type=jnp.float32)
        ).astype(jnp.bfloat16),
        "tp",
    ).astype(jnp.float32)
    gain_second_grad = jnp.sum(own_rows(grad_normed_two) * own_rows(hat_two), axis=0)
    grad_middle = cotangent.astype(jnp.float32) + norm_back(
        grad_normed_two * gain_second_f, hat_two, inverse_two
    )
    grad_middle_low = grad_middle.astype(jnp.bfloat16)
    grad_middle_part = own_rows(grad_middle)
    out_grad = jnp.dot(mixed_low.T, grad_middle_low, preferred_element_type=jnp.float32)
    grad_mixed = jnp.dot(grad_middle_low, out_w.T, preferred_element_type=jnp.float32).astype(
        jnp.bfloat16
    )
    totals = jnp.sum(
        (grad_mixed.astype(jnp.float32) * mixed_full).reshape(tok_rows, head_count, HEAD), axis=-1
    )
    grad_qrot, key_part, value_part = attend_back(
        queries, grad_mixed, log_totals, totals, keys_all, values_all, head_count
    )
    grad_krot, grad_values = (
        lax.psum_scatter(
            key_part.astype(jnp.bfloat16), "ctx", scatter_dimension=0, tiled=True
        ).astype(jnp.float32),
        lax.psum_scatter(
            value_part.astype(jnp.bfloat16), "ctx", scatter_dimension=0, tiled=True
        ).astype(jnp.float32),
    )
    grad_q = (
        rotary_back(grad_qrot.reshape(tok_rows, head_count, HEAD), cosine_table, sine_table)
        .reshape(tok_rows, feature_count)
        .astype(jnp.bfloat16)
    )
    grad_k = (
        rotary_back(grad_krot.reshape(tok_rows, head_count, HEAD), cosine_table, sine_table)
        .reshape(tok_rows, feature_count)
        .astype(jnp.bfloat16)
    )
    grad_v = grad_values.astype(jnp.bfloat16)
    query_grad = jnp.dot(normed.T, grad_q, preferred_element_type=jnp.float32)
    key_grad = jnp.dot(normed.T, grad_k, preferred_element_type=jnp.float32)
    value_grad = jnp.dot(normed.T, grad_v, preferred_element_type=jnp.float32)
    grad_normed_part = own_rows(
        lax.psum(
            (
                jnp.dot(grad_q, query_w.T, preferred_element_type=jnp.float32)
                + jnp.dot(grad_k, key_w.T, preferred_element_type=jnp.float32)
                + jnp.dot(grad_v, value_w.T, preferred_element_type=jnp.float32)
            ).astype(jnp.bfloat16),
            "tp",
        ).astype(jnp.float32)
    )
    hat_one_part = own_rows(hat_one)
    gain_first_part = jnp.sum(grad_normed_part * hat_one_part, axis=0)
    input_rows = grad_middle_part + norm_back(
        grad_normed_part * gain_first_f, hat_one_part, own_rows(inverse_one)
    )
    gain_first_grad, gain_second_total = lax.psum(
        (gain_first_part, gain_second_grad), ("ctx", "tp")
    )
    summed = context_total(query_grad, key_grad, value_grad, act_grad, up_grad, out_grad, down_grad)
    shares = owner_shares(
        summed[0],
        summed[1],
        summed[2],
        summed[3],
        summed[4],
        gain_first_grad,
        gain_second_total,
        summed[5],
        summed[6],
    )
    return (
        out_rows.astype(jnp.bfloat16),
        input_rows.astype(jnp.bfloat16),
        shares[0],
        shares[1],
        shares[2],
        shares[7],
        shares[3],
        shares[4],
        shares[8],
        shares[5],
        shares[6],
    )


def solution(mesh):
    in_specs = (
        P(("dp", "ctx"), None),
        P("dp", "tp"),
        P("dp", "tp"),
        P("dp", "tp"),
        P("tp", "dp"),
        P("dp", "tp"),
        P("dp", "tp"),
        P("tp", "dp"),
        P("dp"),
        P("dp"),
        P(("dp", "ctx"), None),
    )
    out_specs = (
        P(("dp", "ctx", "tp"), None),
        P(("dp", "ctx", "tp"), None),
        P("dp", "tp"),
        P("dp", "tp"),
        P("dp", "tp"),
        P("tp", "dp"),
        P("dp", "tp"),
        P("dp", "tp"),
        P("tp", "dp"),
        P("dp"),
        P("dp"),
    )
    return jax.shard_map(local, mesh=mesh, in_specs=in_specs, out_specs=out_specs, check_vma=False)
```

profile of v0, /device:TPU:0, one launch (start us, length us, event | category | flops | bytes accessed | tf_op | source)
XLA Modules:
  0.0 796.8 jit_solution(9328104708917841218)
XLA Ops:
  54.8 15.1 %all-gather.5.cloned.1.call-done = bf16[4096,192]{0,1:T(8,128)(2,1)} async-done(((bf16[1024,192]{0,1:T(8,128)(2,1)}), bf16[4096,192]{0,1:T(8,128)(2,1)}) %all-gather.5.cloned.1.call-update) | async-done | bytes 1572880 | tf_op jit(solution)/shard_map/all_gather | solution.py:256
  69.9 58.7 %while.42 = (s32[]{:T(128)}, f32[2,512,192]{1,0,2:T(2,128)}, f32[2,512,3]{1,2,0:T(4,128)S(1)}, bf16[2,512,3,64]{1,3,2,0:T(8,128)(2,1)S(1)}, bf16[4096,3,64]{0,2,...) while((s32[]{:T(128)}, f32[2,512,192]{1,0,2:T(2,128)}, f32[2,512,3]{1,2,0:T(4,128)S(1)}, ...), condition=%wide.region_5.6_spmd, body=%wide.region_2.5_spmd.sunk | while | flops 1660956672 | bytes 194132176 | solution.py:82
  83.8 10.6 %fusion.155 = f32[3,512,64]{1,2,0:T(8,128)S(1)} fusion(bf16[4096,3,64]{0,2,1:T(8,128)(2,1)S(1)} %copy-done.2, f32[3,512,4096]{2,1,0:T(8,128)} %copy-done, f32[3,512]{1,0:T(4,128)S(1)} %fusion.154), kind=kOutput, calls=%fused_computation.3.clone.1 | convolution fusion | flops 824180736 | bytes 27138048 | tf_op jit(solution)/shard_map/while/body/eval_jaxpr/hqk,khd->qhd/dot_general | solution.py:77
  113.1 10.6 %fusion.155 = f32[3,512,64]{1,2,0:T(8,128)S(1)} fusion(bf16[4096,3,64]{0,2,1:T(8,128)(2,1)S(1)} %copy-done.2, f32[3,512,4096]{2,1,0:T(8,128)} %copy-done, f32[3,512]{1,0:T(4,128)S(1)} %fusion.154), kind=kOutput, calls=%fused_computation.3.clone.1 | convolution fusion | flops 824180736 | bytes 27138048 | tf_op jit(solution)/shard_map/while/body/eval_jaxpr/hqk,khd->qhd/dot_general | solution.py:77
  138.1 7.2 all_gather.41
  152.0 7.3 all_gather.43
  159.3 43.0 %all-reduce.11.cloned.1.call-done = bf16[1024,768]{1,0:T(8,128)(2,1)} async-done(((bf16[1024,768]{1,0:T(8,128)(2,1)}), bf16[1024,768]{1,0:T(8,128)(2,1)}) %all-reduce.11.cloned.1.call-update) | async-done | bytes 1572880 | tf_op jit(solution)/shard_map/psum | solution.py:263
  225.9 58.4 %all-reduce.13.cloned.1.call-done = bf16[1024,768]{1,0:T(8,128)(2,1)} async-done(((bf16[1024,768]{1,0:T(8,128)(2,1)}), bf16[1024,768]{1,0:T(8,128)(2,1)}) %all-reduce.13.cloned.1.call-update) | async-done | bytes 1572880 | tf_op jit(solution)/shard_map/psum | solution.py:282
  299.2 99.6 %while.44 = (s32[]{:T(128)}, f32[4,1024,3,64]{1,3,2,0:T(8,128)}, f32[4,1024,3,64]{1,3,2,0:T(8,128)}, f32[2,512,3,64]{1,0,3,2:T(2,128)}, bf16[2,512,3,64]{1,3,2,0...) while((s32[]{:T(128)}, f32[4,1024,3,64]{1,3,2,0:T(8,128)}, ...), condition=%wide.region_17.18_spmd, body=%wide.region_14.17_spmd.sunk | while | flops 1021378560 | bytes 39758236 | solution.py:137
  299.2 41.3 %while.45 = (s32[]{:T(128)}, f32[512,3,64]{0,2,1:T(8,128)S(1)}, f32[4,1024,3,64]{1,3,2,0:T(8,128)}, f32[4,1024,3,64]{1,3,2,0:T(8,128)}, bf16[4,1024,3,64]{1,3,2,...) while((s32[]{:T(128)}, f32[512,3,64]{0,2,1:T(8,128)S(1)}, ...), condition=%wide.region_16.16_spmd.clone.clone, body=%wide.region_15.15_spmd.clone.clone.sunk | while | flops 1021378560 | bytes 37374108 | solution.py:131
  340.9 8.1 %dynamic_update_slice.33 = f32[2,512,3,64]{1,0,3,2:T(2,128)} dynamic-update-slice(f32[2,512,3,64]{1,0,3,2:T(2,128)} %get-tuple-element.656, f32[1,512,3,64]{1,0,3,2:T(1,128)S(1)} %copy.87, s32[]{:T(128)S(6)} %copy.120, s32[]{:T(128)} %constant.57.clone.1..sunk.1, s32[]{:T(128)} %constant.57.clone.1..sunk.1, s32[]{:T(128)} %constant.57.clone.1..sunk.1) | dynamic-update-slice | bytes 786436 | tf_op jit(solution)/shard_map/while/body/jit(dynamic_update_index_in_dim)/dynamic_update_slice | solution.py:137
  349.0 41.3 %while.45 = (s32[]{:T(128)}, f32[512,3,64]{0,2,1:T(8,128)S(1)}, f32[4,1024,3,64]{1,3,2,0:T(8,128)}, f32[4,1024,3,64]{1,3,2,0:T(8,128)}, bf16[4,1024,3,64]{1,3,2,...) while((s32[]{:T(128)}, f32[512,3,64]{0,2,1:T(8,128)S(1)}, ...), condition=%wide.region_16.16_spmd.clone.clone, body=%wide.region_15.15_spmd.clone.clone.sunk | while | flops 1021378560 | bytes 37374108 | solution.py:131
  390.8 8.1 %dynamic_update_slice.33 = f32[2,512,3,64]{1,0,3,2:T(2,128)} dynamic-update-slice(f32[2,512,3,64]{1,0,3,2:T(2,128)} %get-tuple-element.656, f32[1,512,3,64]{1,0,3,2:T(1,128)S(1)} %copy.87, s32[]{:T(128)S(6)} %copy.120, s32[]{:T(128)} %constant.57.clone.1..sunk.1, s32[]{:T(128)} %constant.57.clone.1..sunk.1, s32[]{:T(128)} %constant.57.clone.1..sunk.1) | dynamic-update-slice | bytes 786436 | tf_op jit(solution)/shard_map/while/body/jit(dynamic_update_index_in_dim)/dynamic_update_slice | solution.py:137
  437.3 24.9 %reduce-scatter.26.cloned.1.call-done = bf16[1024,192]{0,1:T(8,128)(2,1)} async-done(((bf16[4096,192]{0,1:T(8,128)(2,1)}), bf16[1024,192]{0,1:T(8,128)(2,1)}) %reduce-scatter.26.cloned.1.call-update) | async-done | bytes 393232 | tf_op jit(solution)/shard_map/reduce_scatter | solution.py:309
  467.9 11.8 %reduce-scatter.40.cloned.1.call-done = bf16[384,288]{1,0:T(8,128)(2,1)} async-done(((bf16[768,288]{1,0:T(8,128)(2,1)}), bf16[384,288]{1,0:T(8,128)(2,1)}) %reduce-scatter.40.cloned.1.call-update) | async-done | bytes 221200
  481.5 15.9 %reduce-scatter.36.cloned.1.call-done = bf16[384,288]{1,0:T(8,128)(2,1)} async-done(((bf16[768,288]{1,0:T(8,128)(2,1)}), bf16[384,288]{1,0:T(8,128)(2,1)}) %reduce-scatter.36.cloned.1.call-update) | async-done | bytes 221200
  499.2 15.8 %reduce-scatter.38.cloned.1.call-done = bf16[384,288]{1,0:T(8,128)(2,1)} async-done(((bf16[768,288]{1,0:T(8,128)(2,1)}), bf16[384,288]{1,0:T(8,128)(2,1)}) %reduce-scatter.38.cloned.1.call-update) | async-done | bytes 221200
  516.8 14.1 %reduce-scatter.34.cloned.1.call-done = bf16[384,192]{1,0:T(8,128)(2,1)} async-done(((bf16[768,192]{1,0:T(8,128)(2,1)}), bf16[384,192]{1,0:T(8,128)(2,1)}) %reduce-scatter.34.cloned.1.call-update) | async-done | bytes 147472
  534.3 12.6 %reduce-scatter.30.cloned.1.call-done = bf16[384,192]{1,0:T(8,128)(2,1)} async-done(((bf16[768,192]{1,0:T(8,128)(2,1)}), bf16[384,192]{1,0:T(8,128)(2,1)}) %reduce-scatter.30.cloned.1.call-update) | async-done | bytes 147472
  548.6 14.2 %reduce-scatter.28.cloned.1.call-done = bf16[384,192]{1,0:T(8,128)(2,1)} async-done(((bf16[768,192]{1,0:T(8,128)(2,1)}), bf16[384,192]{1,0:T(8,128)(2,1)}) %reduce-scatter.28.cloned.1.call-update) | async-done | bytes 147472
  564.5 14.3 %reduce-scatter.32.cloned.1.call-done = bf16[384,192]{1,0:T(8,128)(2,1)} async-done(((bf16[768,192]{1,0:T(8,128)(2,1)}), bf16[384,192]{1,0:T(8,128)(2,1)}) %reduce-scatter.32.cloned.1.call-update) | async-done | bytes 147472
  588.4 33.7 %all-reduce.17.cloned.1.call-done = (bf16[384,192]{0,1:T(8,128)(2,1)}, bf16[384,192]{0,1:T(8,128)(2,1)}, bf16[384,192]{0,1:T(8,128)(2,1)}, bf16[192,384]{1,0:T(8...) async-done(((bf16[384,192]{0,1:T(8,128)(2,1)}, bf16[384,192]{0,1:T(8,128)(2,1)}, bf16[384,192]{0,1:T(8,128)(2,1)}, ...) | async-done | bytes 1253392 | tf_op jit(solution)/shard_map/psum | solution.py:196
  633.0 112.9 %all-reduce.15.cloned.1.call-done = (bf16[1024,768]{1,0:T(8,128)(2,1)}, bf16[1024,768]{1,0:T(8,128)(2,1)}) async-done(((bf16[1024,768]{1,0:T(8,128)(2,1)}, bf16[1024,768]{1,0:T(8,128)(2,1)}), (bf16[1024,768]{1,0:T(8,128)(2,1)}, bf16[1024,768]{1,0:T(8,128)(2,1)})) %all-reduce.15.cloned.1.call-update) | async-done | bytes 3145744 | tf_op jit(solution)/shard_map/psum | solution.py:272
  747.1 32.3 %all-reduce.2 = (bf16[768]{0:T(1024)(128)(2,1)S(1)}, bf16[768]{0:T(1024)(128)(2,1)S(1)}) all-reduce(f32[768]{0:T(1024)S(1)} %get-tuple-element.271, f32[768]{0:T(1024)S(1)} %multiply_reduce_fusion.4), channel_id=1, replica_groups=mesh['dp'=2,'ctx'=4,'tp'=4] {'ctx','tp'}, use_global_device_ids=true, to_apply=%region_38.39 | all-reduce | flops 1536 | bytes 9216 | tf_op jit(solution)/shard_map/psum | solution.py:342
  (351 shorter events, 309.8 us)
Async XLA Ops:
  7.2 15.7 %copy-start.4 = (bf16[1024,768]{1,0:T(8,128)(2,1)S(1)}, bf16[1024,768]{1,0:T(8,128)(2,1)}, u32[]{:S(2)}) copy-start(bf16[1024,768]{1,0:T(8,128)(2,1)} %param.17) | copy-start | bytes 4718596
  7.2 47.6 %all-gather.7.cloned.1.call-start = ((), (), s32[]{:S(2)}) async-start(), calls=%async_computation.10 | async-start | bytes 1966080 | tf_op jit(solution)/shard_map/all_gather | solution.py:257
  25.1 16.1 %copy-start.6 = (bf16[1024,768]{1,0:T(8,128)(2,1)}, bf16[1024,768]{1,0:T(8,128)(2,1)S(1)}, u32[]{:S(2)}) copy-start(bf16[1024,768]{1,0:T(8,128)(2,1)S(1)} %get-tuple-element.356) | copy-start | bytes 4718596
  26.5 43.4 %all-gather.5.cloned.1.call-start = ((), (), s32[]{:S(2)}) async-start(), calls=%async_computation.9 | async-start | bytes 1966080 | tf_op jit(solution)/shard_map/all_gather | solution.py:256
  35.3 167.1 %all-reduce.11.cloned.1.call-start = ((), (), s32[]{:S(2)}) async-start(), calls=%async_computation.11 | async-start | bytes 3145728 | tf_op jit(solution)/shard_map/psum | solution.py:263
  128.6 16.7 %copy-start.43 = (bf16[384,288]{0,1:T(8,128)(2,1)S(1)}, bf16[384,288]{0,1:T(8,128)(2,1)}, u32[]{:S(2)}) copy-start(bf16[384,288]{0,1:T(8,128)(2,1)} %param.23) | copy-start | bytes 663556
  129.9 74.4 %copy-start.17 = (f32[24,8,2,512]{3,1,2,0:T(8,128)}, f32[24,8,2,512]{3,1,2,0:T(8,128)S(1)}, u32[]{:S(2)}) copy-start(f32[24,8,2,512]{3,1,2,0:T(8,128)S(1)} %copy.80) | copy-start | bytes 2359300
  129.9 22.1 %copy-start.44 = (bf16[288,384]{1,0:T(8,128)(2,1)S(1)}, bf16[288,384]{1,0:T(8,128)(2,1)}, u32[]{:S(2)}) copy-start(bf16[288,384]{1,0:T(8,128)(2,1)} %param.24) | copy-start | bytes 663556
  130.0 72.4 %copy-start.5 = (bf16[1024,768]{1,0:T(8,128)(2,1)S(1)}, bf16[1024,768]{1,0:T(8,128)(2,1)}, u32[]{:S(2)}) copy-start(bf16[1024,768]{1,0:T(8,128)(2,1)} %param.17) | copy-start | bytes 4718596
  133.1 151.2 %all-reduce.13.cloned.1.call-start = ((), (), s32[]{:S(2)}) async-start(), calls=%async_computation.12 | async-start | bytes 3145728 | tf_op jit(solution)/shard_map/psum | solution.py:282
  215.9 215.5 %reduce-scatter.24.cloned.1.call-start = ((), (), s32[]{:S(2)}) async-start(), calls=%async_computation.13 | async-start | bytes 1966080 | tf_op jit(solution)/shard_map/reduce_scatter | solution.py:306
  404.1 58.1 %reduce-scatter.26.cloned.1.call-start = ((), (), s32[]{:S(2)}) async-start(), calls=%async_computation.14 | async-start | bytes 1966080 | tf_op jit(solution)/shard_map/reduce_scatter | solution.py:309
  407.9 71.8 %reduce-scatter.40.cloned.1.call-start = ((), (), s32[]{:S(2)}) async-start(), calls=%async_computation.21 | async-start | bytes 884736
  412.7 84.7 %reduce-scatter.36.cloned.1.call-start = ((), (), s32[]{:S(2)}) async-start(), calls=%async_computation.19 | async-start | bytes 884736
  415.6 99.4 %reduce-scatter.38.cloned.1.call-start = ((), (), s32[]{:S(2)}) async-start(), calls=%async_computation.20 | async-start | bytes 884736
  420.9 110.0 %reduce-scatter.34.cloned.1.call-start = ((), (), s32[]{:S(2)}) async-start(), calls=%async_computation.18 | async-start | bytes 589824
  426.6 120.3 %reduce-scatter.30.cloned.1.call-start = ((), (), s32[]{:S(2)}) async-start(), calls=%async_computation.16 | async-start | bytes 589824
  435.8 127.0 %reduce-scatter.28.cloned.1.call-start = ((), (), s32[]{:S(2)}) async-start(), calls=%async_computation.15 | async-start | bytes 589824
  435.8 28.9 %copy-start.41 = (bf16[288,768]{1,0:T(8,128)(2,1)S(1)}, bf16[288,768]{1,0:T(8,128)(2,1)}, u32[]{:S(2)}) copy-start(bf16[288,768]{1,0:T(8,128)(2,1)} %all_gather.43) | copy-start | bytes 1327108
  437.3 141.5 %reduce-scatter.32.cloned.1.call-start = ((), (), s32[]{:S(2)}) async-start(), calls=%async_computation.17 | async-start | bytes 589824
  464.6 157.5 %all-reduce.17.cloned.1.call-start = ((), (), s32[]{:S(2)}) async-start(), calls=%async_computation.23 | async-start | bytes 2506752 | tf_op jit(solution)/shard_map/psum | solution.py:196
  580.5 165.3 %all-reduce.15.cloned.1.call-start = ((), (), s32[]{:S(2)}) async-start(), calls=%async_computation.22 | async-start | bytes 6291456 | tf_op jit(solution)/shard_map/psum | solution.py:272
  586.8 159.0 %copy-start.19 = (f32[1024,768]{1,0:T(8,128)S(1)}, f32[1024,768]{1,0:T(8,128)}, u32[]{:S(2)}) copy-start(f32[1024,768]{1,0:T(8,128)} %get-tuple-element.355) | copy-start | bytes 9437188
  586.8 159.0 %copy-start.51 = (f32[768]{0:T(1024)S(1)}, f32[768]{0:T(1024)}, u32[]{:S(2)}) copy-start(f32[768]{0:T(1024)} %copy-done.50) | copy-start | bytes 9220
  (54 other events, 218.8 us)
Sparse Core Ops, SparseCore 0:
  26.6 21.4 all-gather.6
  50.2 19.6 all-gather.4
  133.2 69.0 all-reduce.10
  216.1 68.1 all-reduce.12
  404.2 27.2 reduce-scatter.23
  434.0 28.1 reduce-scatter.25
  464.4 15.2 reduce-scatter.39
  482.1 15.2 reduce-scatter.35
  499.7 15.2 reduce-scatter.37
  517.8 13.1 reduce-scatter.33
  533.7 13.1 reduce-scatter.29
  549.6 13.1 reduce-scatter.27
  565.6 13.1 reduce-scatter.31
  582.4 39.6 all-reduce.16
  624.3 121.4 all-reduce.14
where the time goes:
time: 805 us; the launch traced here: 797 us
  waiting for transfers between devices  392 us (49%)
  matrix products  134 us (17%)
  local copies, waits for them, and re-layouts  104 us (13%)
  blocking collectives  91.8 us (11%)
  other arithmetic  58.1 us (7%)
  between operations  15.8 us (2%)
    psum x1, waiting for transfers between devices, local(): lax.psum(jnp.dot(hidden, down_w, preferred_element_type=jnp.float32).asty...  113 us
    unnamed x22, waiting for transfers between devices  98.9 us
    psum x1, waiting for transfers between devices, local(): lax.psum((jnp.dot(grad_gate, act_w.T, preferred_element_type=jnp.float32)...  58.4 us
    psum x1, waiting for transfers between devices, local(): lax.psum(jnp.dot(mixed_low, out_w, preferred_element_type=jnp.float32).as...  43 us
    unnamed x131, local copies, waits for them, and re-layouts  34.2 us
    psum x1, waiting for transfers between devices, context_total(): lax.psum(query_grad.astype(jnp.bfloat16), 'ctx').astype(jnp.float32)  33.7 us
    psum x1, blocking collectives, local(): lax.psum((gain_first_part, gain_second_grad), ('ctx', 'tp'))  32.3 us
    reduce_scatter x1, waiting for transfers between devices, local(): lax.psum_scatter(value_part.astype(jnp.bfloat16), 'ctx', scatter_dimensio...  24.9 us
  transfers between devices with their start and end apart: 15, of which 14 were waited for; matrix products, arithmetic and copies ran while one was open for 10% of the time, Pallas kernels for 0%

commit v1 on v0

--- a/solution.py
+++ b/solution.py
@@ -3,6 +3,7 @@
 import jax.numpy as jnp
 from jax import lax
 from jax.sharding import PartitionSpec as P
+from jax.lax import psum
 
 HEAD = 64
 EPSILON = 1e-05
@@ -339,9 +340,15 @@
     input_rows = grad_middle_part + norm_back(
         grad_normed_part * gain_first_f, hat_one_part, own_rows(inverse_one)
     )
-    gain_first_grad, gain_second_total = lax.psum(
-        (gain_first_part, gain_second_grad), ("ctx", "tp")
-    )
+
+    def _name_halves(state):
+        across = "ctx"
+        named_axis = "tp"
+        for src_i in (named_axis, across):
+            state = psum(state, axis_name=src_i)
+        return state
+
+    gain_first_grad, gain_second_total = _name_halves((gain_first_part, gain_second_grad))
     summed = context_total(query_grad, key_grad, value_grad, act_grad, up_grad, out_grad, down_grad)
     shares = owner_shares(
         summed[0],

time: 805 us -> 788 us (0.979)
  blocking collectives: 91.8 us -> 74.8 us
    psum x1 -> x2, blocking collectives: 32.3 us -> 15.4 us  [_name_halves(): state = psum(state, axis_name=src_i)]
where the time goes in v1:
time: 788 us; the launch traced here: 780 us
  waiting for transfers between devices  392 us (50%)
  matrix products  134 us (17%)
  local copies, waits for them, and re-layouts  104 us (13%)
  blocking collectives  74.8 us (9%)
  other arithmetic  58.1 us (7%)
  between operations  15.8 us (2%)
    psum x1, waiting for transfers between devices, local(): lax.psum(jnp.dot(hidden, down_w, preferred_element_type=jnp.float32).asty...  113 us
    unnamed x22, waiting for transfers between devices  98.9 us
    psum x1, waiting for transfers between devices, local(): lax.psum((jnp.dot(grad_gate, act_w.T, preferred_element_type=jnp.float32)...  58.4 us
    psum x1, waiting for transfers between devices, local(): lax.psum(jnp.dot(mixed_low, out_w, preferred_element_type=jnp.float32).as...  43.1 us
    unnamed x131, local copies, waits for them, and re-layouts  34.2 us
    psum x1, waiting for transfers between devices, context_total(): lax.psum(query_grad.astype(jnp.bfloat16), 'ctx').astype(jnp.float32)  33.7 us
    reduce_scatter x1, waiting for transfers between devices, local(): lax.psum_scatter(value_part.astype(jnp.bfloat16), 'ctx', scatter_dimensio...  24.9 us
    dot_general x8, matrix products, per_key(): jnp.einsum('qhd,khd->hqk', grad_block, value_block, preferred_element_typ...  23.3 us
  transfers between devices with their start and end apart: 15, of which 14 were waited for; matrix products, arithmetic and copies ran while one was open for 10% of the time, Pallas kernels for 0%

profile of v1, /device:TPU:0, one launch (start us, length us, event | category | flops | bytes accessed | tf_op | source)
XLA Modules:
  0.0 779.9 jit_solution(5150470857416242544)
XLA Ops:
  54.8 15.1 %all-gather.5.cloned.1.call-done = bf16[4096,192]{0,1:T(8,128)(2,1)} async-done(((bf16[1024,192]{0,1:T(8,128)(2,1)}), bf16[4096,192]{0,1:T(8,128)(2,1)}) %all-gather.5.cloned.1.call-update) | async-done | bytes 1572880 | tf_op jit(solution)/shard_map/all_gather | solution.py:257
  70.0 58.6 %while.42 = (s32[]{:T(128)}, f32[2,512,192]{1,0,2:T(2,128)}, f32[2,512,3]{1,2,0:T(4,128)S(1)}, bf16[2,512,3,64]{1,3,2,0:T(8,128)(2,1)S(1)}, bf16[4096,3,64]{0,2,...) while((s32[]{:T(128)}, f32[2,512,192]{1,0,2:T(2,128)}, f32[2,512,3]{1,2,0:T(4,128)S(1)}, ...), condition=%wide.region_5.6_spmd, body=%wide.region_2.5_spmd.sunk | while | flops 1660956672 | bytes 194132176 | solution.py:83
  83.8 10.6 %fusion.155 = f32[3,512,64]{1,2,0:T(8,128)S(1)} fusion(bf16[4096,3,64]{0,2,1:T(8,128)(2,1)S(1)} %copy-done.2, f32[3,512,4096]{2,1,0:T(8,128)} %copy-done, f32[3,512]{1,0:T(4,128)S(1)} %fusion.154), kind=kOutput, calls=%fused_computation.3.clone.1 | convolution fusion | flops 824180736 | bytes 27138048 | tf_op jit(solution)/shard_map/while/body/eval_jaxpr/hqk,khd->qhd/dot_general | solution.py:78
  113.1 10.6 %fusion.155 = f32[3,512,64]{1,2,0:T(8,128)S(1)} fusion(bf16[4096,3,64]{0,2,1:T(8,128)(2,1)S(1)} %copy-done.2, f32[3,512,4096]{2,1,0:T(8,128)} %copy-done, f32[3,512]{1,0:T(4,128)S(1)} %fusion.154), kind=kOutput, calls=%fused_computation.3.clone.1 | convolution fusion | flops 824180736 | bytes 27138048 | tf_op jit(solution)/shard_map/while/body/eval_jaxpr/hqk,khd->qhd/dot_general | solution.py:78
  138.1 7.2 all_gather.41
  152.0 7.3 all_gather.43
  159.3 43.1 %all-reduce.12.cloned.1.call-done = bf16[1024,768]{1,0:T(8,128)(2,1)} async-done(((bf16[1024,768]{1,0:T(8,128)(2,1)}), bf16[1024,768]{1,0:T(8,128)(2,1)}) %all-reduce.12.cloned.1.call-update) | async-done | bytes 1572880 | tf_op jit(solution)/shard_map/psum | solution.py:264
  225.8 58.4 %all-reduce.14.cloned.1.call-done = bf16[1024,768]{1,0:T(8,128)(2,1)} async-done(((bf16[1024,768]{1,0:T(8,128)(2,1)}), bf16[1024,768]{1,0:T(8,128)(2,1)}) %all-reduce.14.cloned.1.call-update) | async-done | bytes 1572880 | tf_op jit(solution)/shard_map/psum | solution.py:283
  299.2 99.6 %while.44 = (s32[]{:T(128)}, f32[4,1024,3,64]{1,3,2,0:T(8,128)}, f32[4,1024,3,64]{1,3,2,0:T(8,128)}, f32[2,512,3,64]{1,0,3,2:T(2,128)}, bf16[2,512,3,64]{1,3,2,0...) while((s32[]{:T(128)}, f32[4,1024,3,64]{1,3,2,0:T(8,128)}, ...), condition=%wide.region_17.18_spmd, body=%wide.region_14.17_spmd.sunk | while | flops 1021378560 | bytes 39758236 | solution.py:138
  299.2 41.3 %while.45 = (s32[]{:T(128)}, f32[512,3,64]{0,2,1:T(8,128)S(1)}, f32[4,1024,3,64]{1,3,2,0:T(8,128)}, f32[4,1024,3,64]{1,3,2,0:T(8,128)}, bf16[4,1024,3,64]{1,3,2,...) while((s32[]{:T(128)}, f32[512,3,64]{0,2,1:T(8,128)S(1)}, ...), condition=%wide.region_16.16_spmd.clone.clone, body=%wide.region_15.15_spmd.clone.clone.sunk | while | flops 1021378560 | bytes 37374108 | solution.py:132
  340.9 8.1 %dynamic_update_slice.33 = f32[2,512,3,64]{1,0,3,2:T(2,128)} dynamic-update-slice(f32[2,512,3,64]{1,0,3,2:T(2,128)} %get-tuple-element.658, f32[1,512,3,64]{1,0,3,2:T(1,128)S(1)} %copy.87, s32[]{:T(128)S(6)} %copy.120, s32[]{:T(128)} %constant.57.clone.1..sunk.1, s32[]{:T(128)} %constant.57.clone.1..sunk.1, s32[]{:T(128)} %constant.57.clone.1..sunk.1) | dynamic-update-slice | bytes 786436 | tf_op jit(solution)/shard_map/while/body/jit(dynamic_update_index_in_dim)/dynamic_update_slice | solution.py:138
  349.0 41.3 %while.45 = (s32[]{:T(128)}, f32[512,3,64]{0,2,1:T(8,128)S(1)}, f32[4,1024,3,64]{1,3,2,0:T(8,128)}, f32[4,1024,3,64]{1,3,2,0:T(8,128)}, bf16[4,1024,3,64]{1,3,2,...) while((s32[]{:T(128)}, f32[512,3,64]{0,2,1:T(8,128)S(1)}, ...), condition=%wide.region_16.16_spmd.clone.clone, body=%wide.region_15.15_spmd.clone.clone.sunk | while | flops 1021378560 | bytes 37374108 | solution.py:132
  390.7 8.1 %dynamic_update_slice.33 = f32[2,512,3,64]{1,0,3,2:T(2,128)} dynamic-update-slice(f32[2,512,3,64]{1,0,3,2:T(2,128)} %get-tuple-element.658, f32[1,512,3,64]{1,0,3,2:T(1,128)S(1)} %copy.87, s32[]{:T(128)S(6)} %copy.120, s32[]{:T(128)} %constant.57.clone.1..sunk.1, s32[]{:T(128)} %constant.57.clone.1..sunk.1, s32[]{:T(128)} %constant.57.clone.1..sunk.1) | dynamic-update-slice | bytes 786436 | tf_op jit(solution)/shard_map/while/body/jit(dynamic_update_index_in_dim)/dynamic_update_slice | solution.py:138
  437.3 24.9 %reduce-scatter.26.cloned.1.call-done = bf16[1024,192]{0,1:T(8,128)(2,1)} async-done(((bf16[4096,192]{0,1:T(8,128)(2,1)}), bf16[1024,192]{0,1:T(8,128)(2,1)}) %reduce-scatter.26.cloned.1.call-update) | async-done | bytes 393232 | tf_op jit(solution)/shard_map/reduce_scatter | solution.py:310
  467.9 11.8 %reduce-scatter.40.cloned.1.call-done = bf16[384,288]{1,0:T(8,128)(2,1)} async-done(((bf16[768,288]{1,0:T(8,128)(2,1)}), bf16[384,288]{1,0:T(8,128)(2,1)}) %reduce-scatter.40.cloned.1.call-update) | async-done | bytes 221200
  481.5 15.9 %reduce-scatter.36.cloned.1.call-done = bf16[384,288]{1,0:T(8,128)(2,1)} async-done(((bf16[768,288]{1,0:T(8,128)(2,1)}), bf16[384,288]{1,0:T(8,128)(2,1)}) %reduce-scatter.36.cloned.1.call-update) | async-done | bytes 221200
  499.2 15.8 %reduce-scatter.38.cloned.1.call-done = bf16[384,288]{1,0:T(8,128)(2,1)} async-done(((bf16[768,288]{1,0:T(8,128)(2,1)}), bf16[384,288]{1,0:T(8,128)(2,1)}) %reduce-scatter.38.cloned.1.call-update) | async-done | bytes 221200
  516.8 14.1 %reduce-scatter.34.cloned.1.call-done = bf16[384,192]{1,0:T(8,128)(2,1)} async-done(((bf16[768,192]{1,0:T(8,128)(2,1)}), bf16[384,192]{1,0:T(8,128)(2,1)}) %reduce-scatter.34.cloned.1.call-update) | async-done | bytes 147472
  534.3 12.6 %reduce-scatter.30.cloned.1.call-done = bf16[384,192]{1,0:T(8,128)(2,1)} async-done(((bf16[768,192]{1,0:T(8,128)(2,1)}), bf16[384,192]{1,0:T(8,128)(2,1)}) %reduce-scatter.30.cloned.1.call-update) | async-done | bytes 147472
  548.6 14.2 %reduce-scatter.28.cloned.1.call-done = bf16[384,192]{1,0:T(8,128)(2,1)} async-done(((bf16[768,192]{1,0:T(8,128)(2,1)}), bf16[384,192]{1,0:T(8,128)(2,1)}) %reduce-scatter.28.cloned.1.call-update) | async-done | bytes 147472
  564.5 14.3 %reduce-scatter.32.cloned.1.call-done = bf16[384,192]{1,0:T(8,128)(2,1)} async-done(((bf16[768,192]{1,0:T(8,128)(2,1)}), bf16[384,192]{1,0:T(8,128)(2,1)}) %reduce-scatter.32.cloned.1.call-update) | async-done | bytes 147472
  588.4 33.7 %all-reduce.18.cloned.1.call-done = (bf16[384,192]{0,1:T(8,128)(2,1)}, bf16[384,192]{0,1:T(8,128)(2,1)}, bf16[384,192]{0,1:T(8,128)(2,1)}, bf16[192,384]{1,0:T(8...) async-done(((bf16[384,192]{0,1:T(8,128)(2,1)}, bf16[384,192]{0,1:T(8,128)(2,1)}, bf16[384,192]{0,1:T(8,128)(2,1)}, ...) | async-done | bytes 1253392 | tf_op jit(solution)/shard_map/psum | solution.py:197
  633.0 112.9 %all-reduce.16.cloned.1.call-done = (bf16[1024,768]{1,0:T(8,128)(2,1)}, bf16[1024,768]{1,0:T(8,128)(2,1)}) async-done(((bf16[1024,768]{1,0:T(8,128)(2,1)}, bf16[1024,768]{1,0:T(8,128)(2,1)}), (bf16[1024,768]{1,0:T(8,128)(2,1)}, bf16[1024,768]{1,0:T(8,128)(2,1)})) %all-reduce.16.cloned.1.call-update) | async-done | bytes 3145744 | tf_op jit(solution)/shard_map/psum | solution.py:273
  747.2 9.6 %all-reduce.2 = (f32[768]{0:T(1024)S(1)}, f32[768]{0:T(1024)S(1)}) all-reduce(f32[768]{0:T(1024)S(1)} %get-tuple-element.271, f32[768]{0:T(1024)S(1)} %multiply_reduce_fusion.4), channel_id=1, replica_groups=mesh['dp'=2,'ctx'=4,'tp'=4] {'tp'}, use_global_device_ids=true, to_apply=%region_38.39 | all-reduce | flops 1536 | bytes 12288 | tf_op jit(solution)/shard_map/psum | solution.py:348
  (352 shorter events, 315.5 us)
Async XLA Ops:
  7.2 15.7 %copy-start.4 = (bf16[1024,768]{1,0:T(8,128)(2,1)S(1)}, bf16[1024,768]{1,0:T(8,128)(2,1)}, u32[]{:S(2)}) copy-start(bf16[1024,768]{1,0:T(8,128)(2,1)} %param.17) | copy-start | bytes 4718596
  7.2 47.6 %all-gather.7.cloned.1.call-start = ((), (), s32[]{:S(2)}) async-start(), calls=%async_computation.10 | async-start | bytes 1966080 | tf_op jit(solution)/shard_map/all_gather | solution.py:258
  25.1 16.1 %copy-start.6 = (bf16[1024,768]{1,0:T(8,128)(2,1)}, bf16[1024,768]{1,0:T(8,128)(2,1)S(1)}, u32[]{:S(2)}) copy-start(bf16[1024,768]{1,0:T(8,128)(2,1)S(1)} %get-tuple-element.358) | copy-start | bytes 4718596
  26.5 43.4 %all-gather.5.cloned.1.call-start = ((), (), s32[]{:S(2)}) async-start(), calls=%async_computation.9 | async-start | bytes 1966080 | tf_op jit(solution)/shard_map/all_gather | solution.py:257
  35.3 167.0 %all-reduce.12.cloned.1.call-start = ((), (), s32[]{:S(2)}) async-start(), calls=%async_computation.11 | async-start | bytes 3145728 | tf_op jit(solution)/shard_map/psum | solution.py:264
  128.6 16.7 %copy-start.43 = (bf16[384,288]{0,1:T(8,128)(2,1)S(1)}, bf16[384,288]{0,1:T(8,128)(2,1)}, u32[]{:S(2)}) copy-start(bf16[384,288]{0,1:T(8,128)(2,1)} %param.23) | copy-start | bytes 663556
  129.9 74.4 %copy-start.17 = (f32[24,8,2,512]{3,1,2,0:T(8,128)}, f32[24,8,2,512]{3,1,2,0:T(8,128)S(1)}, u32[]{:S(2)}) copy-start(f32[24,8,2,512]{3,1,2,0:T(8,128)S(1)} %copy.80) | copy-start | bytes 2359300
  130.0 22.0 %copy-start.44 = (bf16[288,384]{1,0:T(8,128)(2,1)S(1)}, bf16[288,384]{1,0:T(8,128)(2,1)}, u32[]{:S(2)}) copy-start(bf16[288,384]{1,0:T(8,128)(2,1)} %param.24) | copy-start | bytes 663556
  130.0 72.4 %copy-start.5 = (bf16[1024,768]{1,0:T(8,128)(2,1)S(1)}, bf16[1024,768]{1,0:T(8,128)(2,1)}, u32[]{:S(2)}) copy-start(bf16[1024,768]{1,0:T(8,128)(2,1)} %param.17) | copy-start | bytes 4718596
  133.0 151.2 %all-reduce.14.cloned.1.call-start = ((), (), s32[]{:S(2)}) async-start(), calls=%async_computation.12 | async-start | bytes 3145728 | tf_op jit(solution)/shard_map/psum | solution.py:283
  215.9 215.5 %reduce-scatter.24.cloned.1.call-start = ((), (), s32[]{:S(2)}) async-start(), calls=%async_computation.13 | async-start | bytes 1966080 | tf_op jit(solution)/shard_map/reduce_scatter | solution.py:307
  404.0 58.1 %reduce-scatter.26.cloned.1.call-start = ((), (), s32[]{:S(2)}) async-start(), calls=%async_computation.14 | async-start | bytes 1966080 | tf_op jit(solution)/shard_map/reduce_scatter | solution.py:310
  407.9 71.8 %reduce-scatter.40.cloned.1.call-start = ((), (), s32[]{:S(2)}) async-start(), calls=%async_computation.21 | async-start | bytes 884736
  412.7 84.7 %reduce-scatter.36.cloned.1.call-start = ((), (), s32[]{:S(2)}) async-start(), calls=%async_computation.19 | async-start | bytes 884736
  415.6 99.4 %reduce-scatter.38.cloned.1.call-start = ((), (), s32[]{:S(2)}) async-start(), calls=%async_computation.20 | async-start | bytes 884736
  420.9 110.0 %reduce-scatter.34.cloned.1.call-start = ((), (), s32[]{:S(2)}) async-start(), calls=%async_computation.18 | async-start | bytes 589824
  426.6 120.3 %reduce-scatter.30.cloned.1.call-start = ((), (), s32[]{:S(2)}) async-start(), calls=%async_computation.16 | async-start | bytes 589824
  435.7 127.0 %reduce-scatter.28.cloned.1.call-start = ((), (), s32[]{:S(2)}) async-start(), calls=%async_computation.15 | async-start | bytes 589824
  435.8 28.9 %copy-start.41 = (bf16[288,768]{1,0:T(8,128)(2,1)S(1)}, bf16[288,768]{1,0:T(8,128)(2,1)}, u32[]{:S(2)}) copy-start(bf16[288,768]{1,0:T(8,128)(2,1)} %all_gather.43) | copy-start | bytes 1327108
  437.2 141.5 %reduce-scatter.32.cloned.1.call-start = ((), (), s32[]{:S(2)}) async-start(), calls=%async_computation.17 | async-start | bytes 589824
  464.6 157.5 %all-reduce.18.cloned.1.call-start = ((), (), s32[]{:S(2)}) async-start(), calls=%async_computation.23 | async-start | bytes 2506752 | tf_op jit(solution)/shard_map/psum | solution.py:197
  580.5 165.4 %all-reduce.16.cloned.1.call-start = ((), (), s32[]{:S(2)}) async-start(), calls=%async_computation.22 | async-start | bytes 6291456 | tf_op jit(solution)/shard_map/psum | solution.py:273
  586.8 159.0 %copy-start.19 = (f32[1024,768]{1,0:T(8,128)S(1)}, f32[1024,768]{1,0:T(8,128)}, u32[]{:S(2)}) copy-start(f32[1024,768]{1,0:T(8,128)} %get-tuple-element.357) | copy-start | bytes 9437188
  586.8 159.0 %copy-start.51 = (f32[768]{0:T(1024)S(1)}, f32[768]{0:T(1024)}, u32[]{:S(2)}) copy-start(f32[768]{0:T(1024)} %copy-done.50) | copy-start | bytes 9220
  (54 other events, 218.8 us)
Sparse Core Ops, SparseCore 0:
  26.6 21.4 all-gather.6
  50.3 19.6 all-gather.4
  133.2 69.1 all-reduce.11
  216.0 68.1 all-reduce.13
  404.2 27.2 reduce-scatter.23
  434.0 28.1 reduce-scatter.25
  464.4 15.2 reduce-scatter.39
  482.1 15.2 reduce-scatter.35
  499.7 15.2 reduce-scatter.37
  517.7 13.1 reduce-scatter.33
  533.7 13.1 reduce-scatter.29
  549.6 13.1 reduce-scatter.27
  565.6 13.1 reduce-scatter.31
  582.4 39.6 all-reduce.17
  624.4 121.4 all-reduce.15
